TPU v7x, 32 devices: a whole 2x2x4 slice. The times are simulated.
32 devices in a mesh: shard: 4 (over z), group: 8 (over y, x, core).
Axes of the slice: x: 2, y: 2, z: 4, core: 2. Of those that a mesh axis runs over, the one named last changes fastest.
Arguments:
- momentum: bfloat16 [32, 1024, 512], P('group', 'shard'), may hold values from -40 to 40
- gradient: bfloat16 [32, 1024, 512], P('group', 'shard'), may hold values from -300 to 300
- weights: bfloat16 [32, 1024, 512], P('group', 'shard'), may hold values from -0.1875 to 0.1875
- slot_map: int32 [8, 4], P('group'), may hold values from 0 to 1, as said below
- tokens: bfloat16 [4, 8, 256, 1024], P('shard', 'group'), may hold values from -6 to 6
Outputs:
- fresh_state: bfloat16 [32, 1024, 512], P('group', 'shard')
- hidden: bfloat16 [4, 8, 256, 512], P('shard', 'group')
Inputs may be any that keep to these rules, and one draw needn't show every extreme that they name: `slot_map`: each row holds every expert-layer of its group at least once and at most four times.
All inputs are finite; a program needn't handle non-finite values.
Results may differ from a plain program's by a relative error of at most 0.014.
Values may be sent and summed in bfloat16 or wider, within the bound.
A program may use at most 64 MiB of HBM per device.

v0:
```python
import math

import jax
import jax.numpy as jnp
from jax import lax
from jax.sharding import PartitionSpec as P

D = 1024
F = 512
ITERS = 5


coefficients = (3.4445, -4.775, 2.0315)
momentum_decay = 0.95
learning_rate = 0.05
clip_rms = 0.5


def orthogonal(matrix):
    widened = matrix.astype(jnp.float32)
    inverse_norm = 1.0 / (jnp.sqrt(jnp.sum(widened * widened)) + 1e-07)
    iterate = (widened * inverse_norm).astype(jnp.bfloat16)
    for iteration in range(ITERS):
        gram = lax.dot_general(
            iterate, iterate, (((0,), (0,)), ((), ())), preferred_element_type=jnp.float32
        ).astype(jnp.bfloat16)
        squared = jnp.dot(gram, gram, preferred_element_type=jnp.float32)
        polynomial = (
            coefficients[1] * gram.astype(jnp.float32) + coefficients[2] * squared
        ).astype(jnp.bfloat16)
        product = jnp.dot(iterate, polynomial, preferred_element_type=jnp.float32)
        iterate = (coefficients[0] * iterate.astype(jnp.float32) + product).astype(jnp.bfloat16)
    return (0.2 * math.sqrt(D) * iterate.astype(jnp.float32)).astype(jnp.bfloat16)


def local(momentum, gradient, weights, slot_map, tokens):
    owners = lax.axis_size("shard")
    every_entry = owners * lax.axis_size("group") * D * F
    widened = gradient.astype(jnp.float32)
    grand_total = lax.psum(jnp.sum(widened * widened), ("shard", "group"))
    clip_factor = jnp.minimum(
        1.0, clip_rms * math.sqrt(every_entry) / jnp.sqrt(grand_total + 1e-06)
    )
    fresh_state = (momentum_decay * momentum.astype(jnp.float32) + clip_factor * widened).astype(
        jnp.bfloat16
    )
    mixed = lax.all_to_all(fresh_state, "shard", split_axis=0, concat_axis=1, tiled=True)[0]
    update = orthogonal(mixed)
    update_rows = lax.all_to_all(update[None], "shard", split_axis=1, concat_axis=0, tiled=True)
    new_weights = (
        weights.astype(jnp.float32) - learning_rate * update_rows.astype(jnp.float32)
    ).astype(jnp.bfloat16)
    paired = new_weights.reshape(owners // 2, 2, new_weights.shape[1], new_weights.shape[2])
    picked = jnp.take(paired, slot_map[0], axis=0)
    slot_pair = lax.all_to_all(picked, "shard", split_axis=0, concat_axis=2, tiled=True)[0]
    prompt = tokens[0, 0]
    gate_out = jnp.dot(prompt, slot_pair[0], preferred_element_type=jnp.float32)
    up_out = jnp.dot(prompt, slot_pair[1], preferred_element_type=jnp.float32)
    hidden = (jax.nn.silu(gate_out) * up_out).astype(jnp.bfloat16)
    return (fresh_state, hidden[None, None])


def solution(mesh):
    in_specs = (
        P("group", "shard", None),
        P("group", "shard", None),
        P("group", "shard", None),
        P("group", None),
        P("shard", "group", None, None),
    )
    out_specs = (P("group", "shard", None), P("shard", "group", None, None))
    return jax.shard_map(local, mesh=mesh, in_specs=in_specs, out_specs=out_specs, check_vma=False)
```

profile of v0, /device:TPU:0, one launch (start us, length us, event | category | flops | bytes accessed | tf_op | source)
XLA Modules:
  0.0 197.2 jit_solution(14266723060621643427)
XLA Ops:
  0.6 2.4 %fusion = f32[]{:T(128)} fusion(bf16[4,256,512]{2,1,0:T(8,128)(2,1)} %param.6), kind=kLoop, calls=%fused_computation.5 | loop fusion | flops 1572863 | bytes 1048580 | tf_op jit(solution)/shard_map/reduce_sum | solution.py:40
  3.1 42.2 %psum.7 = f32[]{:T(128)} all-reduce(f32[]{:T(128)} %fusion), channel_id=1, replica_groups=mesh['shard'=4,'group'=8] {'shard','group'}, use_global_device_ids=true, to_apply=%region_1.0 | all-reduce | flops 1 | bytes 8 | tf_op jit(solution)/shard_map/psum | solution.py:40
  46.0 1.9 fusion.2
  47.9 1.0 copy-done.1
  48.9 28.5 %all_to_all.33 = bf16[4,256,512]{2,1,0:T(8,128)(2,1)S(1)} all-to-all(bf16[4,256,512]{2,1,0:T(8,128)(2,1)S(1)} %fusion.2), channel_id=1, replica_groups=mesh['shard'=4,'group'=8] {'shard'}, dimensions={0} | all-to-all | bytes 2097152 | tf_op jit(solution)/shard_map/all_to_all | solution.py:47
  77.4 1.1 fusion.3
  79.5 0.7 fusion.11
  80.2 1.1 add_convert_fusion.4
  81.3 0.7 convolution_convert_fusion.3
  82.0 1.1 add_convert_fusion.3
  83.1 0.7 convolution_convert_fusion.2
  83.8 1.1 add_convert_fusion.2
  84.9 0.7 convolution_convert_fusion.1
  85.6 1.1 add_convert_fusion.1
  86.7 0.7 convolution_convert_fusion
  87.4 2.1 %fusion.5 = bf16[1,1024,512]{2,1,0:T(8,128)(2,1)} fusion(bf16[1024,512]{1,0:T(8,128)(2,1)S(1)} %add_convert_fusion.1, bf16[512,512]{1,0:T(8,128)(2,1)S(1)} %convolution_convert_fusion), kind=kOutput, calls=%fused_computation.19 | convolution fusion | flops 810287104 | bytes 2621440 | tf_op jit(solution)/shard_map/dot_general | solution.py:31
  89.5 2.8 %copy.15 = bf16[1,1024,512]{2,0,1:T(2,128)(2,1)S(1)} copy(bf16[1,1024,512]{2,1,0:T(8,128)(2,1)} %fusion.5) | data formatting | bytes 2097152 | tf_op jit(solution)/shard_map/broadcast_in_dim | solution.py:49
  92.4 0.5 broadcast.102
  92.9 8.3 %reduce.3 = bf16[1024,512]{1,0:T(8,128)(2,1)} reduce(bf16[1024,1,512]{2,1,0:T(2,128)(2,1)S(1)} %bitcast.70, bf16[]{:T(256)} %broadcast.102), dimensions={1}, to_apply=%bitcast.68.reduce_sub_computation | reduce | bytes 2097154
  101.1 3.7 %reshape.80 = bf16[4,2,65536]{2,1,0:T(2,128)(2,1)} reshape(bf16[1024,512]{1,0:T(8,128)(2,1)} %reduce.3) | data formatting | bytes 2097152
  104.9 4.3 %all-to-all-start.1 = ((bf16[4,2,65536]{2,1,0:T(2,128)(2,1)}), bf16[4,2,65536]{2,1,0:T(2,128)(2,1)}, u32[]{:S(2)}, u32[]{:S(2)}) async-start(bf16[4,2,65536]{2,1,0:T(2,128)(2,1)} %reshape.80), calls=%async_computation.1 | async-start | bytes 2097152 | tf_op jit(solution)/shard_map/all_to_all | solution.py:49
  109.2 24.8 %all-to-all-done.1 = bf16[4,2,65536]{2,1,0:T(2,128)(2,1)} async-done(((bf16[4,2,65536]{2,1,0:T(2,128)(2,1)}), bf16[4,2,65536]{2,1,0:T(2,128)(2,1)}, u32[]{:S(2)}, u32[]{:S(2)}) %all-to-all-start.1) | async-done | bytes 1048608 | tf_op jit(solution)/shard_map/all_to_all | solution.py:49
  134.0 2.6 %reshape.81 = bf16[1024,1,512]{2,1,0:T(2,128)(2,1)S(1)} reshape(bf16[4,2,65536]{2,1,0:T(2,128)(2,1)} %all-to-all-done.1) | data formatting | bytes 2097152
  136.6 2.9 %convert_multiply_fusion.4 = f32[1,1024,512]{2,0,1:T(1,128)S(1)} fusion(bf16[1024,1,512]{2,1,0:T(2,128)(2,1)S(1)} %reshape.81), kind=kLoop, calls=%fused_computation.11 | loop fusion | flops 1048576 | bytes 3145728 | tf_op jit(solution)/shard_map/mul | solution.py:51
  139.7 1.0 copy-done.2
  140.7 0.4 subtract_convert_fusion
  141.1 2.0 %gather_fusion = bf16[4,2,256,512]{3,2,1,0:T(8,128)(2,1)} fusion(bf16[2,2,256,512]{3,2,1,0:T(8,128)(2,1)S(1)} %bitcast.69, s32[1024]{0:T(1024)S(1)} %pad_clamp_fusion), kind=kCustom, calls=%fused_computation | custom fusion | bytes 4194320 | tf_op jit(solution)/shard_map/jit(_take)/gather | solution.py:54
  143.1 1.9 broadcast_select_fusion
  145.0 50.2 %all_to_all.34 = bf16[4,2,256,512]{3,2,1,0:T(8,128)(2,1)S(1)} all-to-all(bf16[4,2,256,512]{3,2,1,0:T(8,128)(2,1)S(1)} %broadcast_select_fusion), channel_id=1, replica_groups=mesh['shard'=4,'group'=8] {'shard'}, dimensions={0} | all-to-all | bytes 4194304 | tf_op jit(solution)/shard_map/all_to_all | solution.py:55
  195.3 0.5 convolution_bitcast_fusion.2
  195.8 0.5 fusion.19
  196.3 0.8 copy.11
  (12 shorter events, 0.5 us)
Async XLA Ops:
  0.6 194.7 %copy-start = (bf16[1,1,256,1024]{3,2,1,0:T(8,128)(2,1)S(1)}, bf16[1,1,256,1024]{3,2,1,0:T(8,128)(2,1)}, u32[]{:S(2)}) copy-start(bf16[1,1,256,1024]{3,2,1,0:T(8,128)(2,1)} %param.9) | copy-start | bytes 1572868
  47.9 1.0 copy-start.1
  101.1 8.0 %copy-start.3 = (s32[1,4]{1,0:T(1,128)S(1)}, s32[1,4]{1,0:T(1,128)}, u32[]{:S(2)}) copy-start(s32[1,4]{1,0:T(1,128)} %param.8) | copy-start | bytes 52
  104.9 29.1 %all-to-all-start.1 = ((bf16[4,2,65536]{2,1,0:T(2,128)(2,1)}), bf16[4,2,65536]{2,1,0:T(2,128)(2,1)}, u32[]{:S(2)}, u32[]{:S(2)}) async-start(bf16[4,2,65536]{2,1,0:T(2,128)(2,1)} %reshape.80), calls=%async_computation.1 | async-start | bytes 2097152 | tf_op jit(solution)/shard_map/all_to_all | solution.py:49
  139.5 1.2 copy-start.2
where the time goes:
time: 198 us; the launch traced here: 197 us
  blocking collectives  121 us (61%)
  waiting for transfers between devices  24.8 us (13%)
  other arithmetic  19 us (10%)
  local copies, waits for them, and re-layouts  14.9 us (8%)
  matrix products  11 us (6%)
  starting transfers between devices  4.26 us (2%)
  between operations  2.26 us (1%)
    all_to_all x1, blocking collectives, local(): lax.all_to_all(picked, 'shard', split_axis=0, concat_axis=2, tiled=True)[0]  50.2 us
    psum x1, blocking collectives, local(): grand_total = lax.psum(jnp.sum(widened * widened), ('shard', 'group'))  42.2 us
    all_to_all x1, blocking collectives, local(): lax.all_to_all(fresh_state, 'shard', split_axis=0, concat_axis=1, tiled=T...  28.5 us
    all_to_all x1, waiting for transfers between devices, local(): lax.all_to_all(update[None], 'shard', split_axis=1, concat_axis=0, tiled=...  24.8 us
    unnamed x13, local copies, waits for them, and re-layouts  9.92 us
    unnamed x1, other arithmetic  8.25 us
    dot_general x5, matrix products, orthogonal(): product = jnp.dot(iterate, polynomial, preferred_element_type=jnp.float32)  6.29 us
    all_to_all x1, starting transfers between devices, local(): lax.all_to_all(update[None], 'shard', split_axis=1, concat_axis=0, tiled=...  4.26 us
  transfers between devices with their start and end apart: 1, of which 1 were waited for; matrix products, arithmetic and copies ran while one was open for 0% of the time, Pallas kernels for 0%

commit v1 on v0

v1 whole, which is shorter than its diff:
```python
import functools
import math

import jax
import jax.numpy as jnp
from jax import lax
from jax.experimental import pallas as pl
from jax.experimental.pallas import tpu as pltpu
from jax.sharding import PartitionSpec as P

ITERS = 5
coefficients = (3.4445, -4.775, 2.0315)
momentum_decay = 0.95
learning_rate = 0.05
clip_rms = 0.5
MESH = pl.DeviceIdType.MESH
f32, bf16 = jnp.float32, jnp.bfloat16


def kernel(
    n, groups, slot_ref, mom_ref, grad_ref, w_ref, tok_ref, fresh_ref, hid_ref,
    part, line_sums, group_sums, x_buf, gram_buf, poly_buf, w_buf, tok_buf, nw_buf, hid_send, hid_recv,
    line_s, line_r, group_s, group_r, x_s, x_r, w_s, w_r, tok_s, tok_r, nw_s, nw_r, hid_s, hid_r,
):
    half = n // 2
    z, g = lax.axis_index("shard"), lax.axis_index("group")
    core = lax.rem(g, 2)
    base = g - core
    side, spot = lax.div(z, half), lax.rem(z, half)
    rows, cols = mom_ref.shape[1], mom_ref.shape[2]
    depth = n * rows
    every_entry = n * groups * depth * cols

    def is_me(zz, gg):
        return jnp.logical_and(zz == z, gg == g)

    def remote(src, dst, ssem, rsem, zz, gg):
        return pltpu.make_async_remote_copy(
            src_ref=src, dst_ref=dst, send_sem=ssem, recv_sem=rsem,
            device_id={"shard": zz, "group": gg}, device_id_type=MESH,
        )

    def ship(src, dst, ssem, rsem, zz, gg):
        same = is_me(zz, gg)

        @pl.when(same)
        def _():
            pltpu.make_async_copy(src, dst, rsem).start()

        @pl.when(jnp.logical_not(same))
        def _():
            remote(src, dst, ssem, rsem, zz, gg).start()

    def sent(src, dst, ssem, rsem, zz, gg):
        @pl.when(jnp.logical_not(is_me(zz, gg)))
        def _():
            remote(src, dst, ssem, rsem, zz, gg).wait_send()

    def landed(dst, rsem):
        pltpu.make_async_copy(dst, dst, rsem).wait()

    barrier = pltpu.get_barrier_semaphore()

    def greet(zz, gg):
        pl.semaphore_signal(barrier, inc=1, device_id={"shard": zz, "group": gg}, device_id_type=MESH)

    for step in range(n):
        greet(lax.rem(z + step, n), base + 1 - core)
        if step:
            greet(lax.rem(z + step, n), g)
    for step in range(2, groups):
        greet(z, lax.rem(base + step, groups))

    def squares(i, total):
        wide = grad_ref[i].astype(f32)
        return total + jnp.sum((wide * wide).reshape(rows // 8, 8, cols), axis=0)

    total = lax.fori_loop(0, n, squares, jnp.zeros((8, cols), f32))
    tile = total[:, :128]
    for at in range(128, cols, 128):
        tile = tile + total[:, at : at + 128]
    part[0] = tile
    pl.semaphore_wait(barrier, 2 * n - 1 + groups - 2)

    for step in range(1, n):
        to = lax.rem(z + step, n)
        remote(part.at[0], line_sums.at[z], line_s.at[step], line_r.at[z], to, g).start()
    line_sums[z] = tile
    for step in range(1, n):
        other = lax.rem(z + step, n)
        landed(line_sums.at[other], line_r.at[other])
    part[1] = jnp.sum(line_sums[...], axis=0)
    for step in range(1, groups):
        to = lax.rem(g + step, groups)
        remote(part.at[1], group_sums.at[g], group_s.at[step], group_r.at[g], z, to).start()
    group_sums[g] = part[1]
    for step in range(1, groups):
        other = lax.rem(g + step, groups)
        landed(group_sums.at[other], group_r.at[other])
    grand_total = jnp.sum(jnp.sum(group_sums[...], axis=0), keepdims=True)
    clip = jnp.minimum(1.0, clip_rms * math.sqrt(every_entry) / jnp.sqrt(grand_total + 1e-06))

    def owner(j):
        return core * half + lax.div(j, 2), base + lax.rem(j, 2)

    my_rows = pl.ds(pl.multiple_of(z * rows, rows), rows)

    def row_copy(j):
        return (fresh_ref.at[j], x_buf.at[my_rows], x_s.at[j], x_r.at[z], *owner(j))

    def weight_copy(j):
        return (w_ref.at[j], w_buf.at[my_rows], w_s.at[j], w_r.at[z], *owner(j))

    slot_core = base + side

    def token_copy(i):
        return (tok_ref.at[0, 0], tok_buf.at[spot], tok_s.at[i], tok_r.at[spot], core * half + i, slot_core)

    def every(count, act):
        def body(i, carry):
            act(i)
            return carry

        lax.fori_loop(0, count, body, 0)

    def freshen(j):
        fresh_ref[j] = (momentum_decay * mom_ref[j].astype(f32) + clip * grad_ref[j].astype(f32)).astype(bf16)
        ship(*row_copy(j))

    every(n, freshen)
    every(n, lambda j: ship(*weight_copy(j)))
    every(half, lambda i: ship(*token_copy(i)))

    def block(d):
        return pl.ds(pl.multiple_of(d * rows, rows), rows)

    every(n, lambda d: landed(x_buf.at[block(d)], x_r.at[d]))

    chunk = 256

    def norm_part(i, acc):
        wide = x_buf[pl.ds(pl.multiple_of(i * chunk, chunk), chunk)].astype(f32)
        return acc + jnp.sum((wide * wide).reshape(chunk // 8, 8, cols), axis=0)

    norm = jnp.sum(lax.fori_loop(0, depth // chunk, norm_part, jnp.zeros((8, cols), f32)), keepdims=True)
    inverse_norm = 1.0 / (jnp.sqrt(norm) + 1e-07)

    def scale(i):
        at = pl.ds(pl.multiple_of(i * chunk, chunk), chunk)
        x_buf[at] = (x_buf[at].astype(f32) * inverse_norm).astype(bf16)

    every(depth // chunk, scale)

    def iterate(_):
        x = x_buf[...]
        gram_buf[...] = lax.dot_general(x, x, (((0,), (0,)), ((), ())), preferred_element_type=f32).astype(bf16)
        gram = gram_buf[...]
        squared = jnp.dot(gram, gram, preferred_element_type=f32)
        poly_buf[...] = (coefficients[1] * gram.astype(f32) + coefficients[2] * squared).astype(bf16)
        x = x_buf[...]
        product = jnp.dot(x, poly_buf[...], preferred_element_type=f32)
        x_buf[...] = (coefficients[0] * x.astype(f32) + product).astype(bf16)

    every(ITERS, iterate)

    every(n, lambda d: landed(w_buf.at[block(d)], w_r.at[d]))

    def renew(i):
        at = pl.ds(pl.multiple_of(i * chunk, chunk), chunk)
        update = (0.2 * math.sqrt(depth) * x_buf[at].astype(f32)).astype(bf16)
        nw_buf[core, at] = (w_buf[at].astype(f32) - learning_rate * update.astype(f32)).astype(bf16)

    every(depth // chunk, renew)
    swap = remote(nw_buf.at[core], nw_buf.at[core], nw_s, nw_r.at[core], z, base + 1 - core)
    swap.start()
    landed(nw_buf.at[1 - core], nw_r.at[1 - core])

    def hidden_copy(i):
        return (hid_send.at[i], hid_recv.at[spot], hid_s.at[i], hid_r.at[spot], core * half + i, base + side)

    def prefill(i):
        landed(tok_buf.at[i], tok_r.at[i])
        prompt = tok_buf[i]
        gate = jnp.dot(prompt, nw_buf[0], preferred_element_type=f32)
        up = jnp.dot(prompt, nw_buf[1], preferred_element_type=f32)
        hid_send[i] = (gate / (1.0 + jnp.exp(-gate)) * up).astype(bf16)
        ship(*hidden_copy(i))

    every(half, prefill)
    every(half, lambda q: landed(hid_recv.at[q], hid_r.at[q]))
    hid_ref[0, 0] = hid_recv[slot_ref[0, z]]

    for step in range(1, n):
        remote(part.at[0], line_sums.at[z], line_s.at[step], line_r.at[z], lax.rem(z + step, n), g).wait_send()
    for step in range(1, groups):
        remote(part.at[1], group_sums.at[g], group_s.at[step], group_r.at[g], z, lax.rem(g + step, groups)).wait_send()
    every(n, lambda j: sent(*row_copy(j)))
    every(n, lambda j: sent(*weight_copy(j)))
    every(half, lambda i: sent(*token_copy(i)))
    every(half, lambda i: sent(*hidden_copy(i)))
    swap.wait_send()


def local(n, groups, momentum, gradient, weights, slot_map, tokens):
    rows, cols = momentum.shape[1:]
    depth, half, prompts = n * rows, n // 2, tokens.shape[2]
    vmem = pl.BlockSpec(memory_space=pltpu.VMEM)
    dma = pltpu.SemaphoreType.DMA
    return pl.pallas_call(
        functools.partial(kernel, n, groups),
        out_shape=(
            jax.ShapeDtypeStruct(momentum.shape, bf16),
            jax.ShapeDtypeStruct((1, 1, prompts, cols), bf16),
        ),
        in_specs=[pl.BlockSpec(memory_space=pltpu.SMEM)] + [vmem] * 4,
        out_specs=(vmem, vmem),
        scratch_shapes=[
            pltpu.VMEM((2, 8, 128), f32),
            pltpu.VMEM((n, 8, 128), f32),
            pltpu.VMEM((groups, 8, 128), f32),
            pltpu.VMEM((depth, cols), bf16),
            pltpu.VMEM((cols, cols), bf16),
            pltpu.VMEM((cols, cols), bf16),
            pltpu.VMEM((depth, cols), bf16),
            pltpu.VMEM((half, prompts, depth), bf16),
            pltpu.VMEM((2, depth, cols), bf16),
            pltpu.VMEM((half, prompts, cols), bf16),
            pltpu.VMEM((half, prompts, cols), bf16),
            dma((n,)), dma((n,)), dma((groups,)), dma((groups,)),
            dma((n,)), dma((n,)), dma((n,)), dma((n,)), dma((half,)), dma((half,)),
            dma(()), dma((2,)), dma((half,)), dma((half,)),
        ],
        compiler_params=pltpu.CompilerParams(
            collective_id=0, has_side_effects=True, vmem_limit_bytes=50 * 2**20
        ),
    )(slot_map, momentum, gradient, weights, tokens)


def solution(mesh):
    in_specs = (
        P("group", "shard", None),
        P("group", "shard", None),
        P("group", "shard", None),
        P("group", None),
        P("shard", "group", None, None),
    )
    out_specs = (P("group", "shard", None), P("shard", "group", None, None))
    step = functools.partial(local, mesh.shape["shard"], mesh.shape["group"])
    return jax.shard_map(step, mesh=mesh, in_specs=in_specs, out_specs=out_specs, check_vma=False)
```

time: 198 us -> 101 us (0.51)
  the two profiles are of different devices: /device:TPU:0 before, /device:TPU:9 now
where the time goes in v1:
time: 101 us; the launch traced here: 100 us
  Pallas kernels  93.8 us (93%)
  local copies, waits for them, and re-layouts  5.81 us (6%)
    pallas_call x1, Pallas kernels, local(): pl.pallas_call(functools.partial(kernel, n, groups), out_shape=(jax.Shape...  93.8 us
    unnamed x10, local copies, waits for them, and re-layouts  5.81 us

profile of v1, /device:TPU:9, one launch (start us, length us, event | category | flops | bytes accessed | tf_op | source)
XLA Modules:
  0.0 100.3 jit_solution(16115120175265928016)
XLA Ops:
  0.6 0.0 copy-start
  0.6 1.2 %copy-done = bf16[4,256,512]{2,1,0:T(8,128)(2,1)S(1)} copy-done((bf16[4,256,512]{2,1,0:T(8,128)(2,1)S(1)}, bf16[4,256,512]{2,1,0:T(8,128)(2,1)}, u32[]{:S(2)}) %copy-start) | copy-done | bytes 1048600
  1.9 0.0 copy-start.1
  1.9 1.2 %copy-done.1 = bf16[4,256,512]{2,1,0:T(8,128)(2,1)S(1)} copy-done((bf16[4,256,512]{2,1,0:T(8,128)(2,1)S(1)}, bf16[4,256,512]{2,1,0:T(8,128)(2,1)}, u32[]{:S(2)}) %copy-start.1) | copy-done | bytes 1048600
  3.1 0.0 copy-start.2
  3.1 1.0 %copy-done.2 = bf16[1,1,256,1024]{3,2,1,0:T(8,128)(2,1)S(1)} copy-done((bf16[1,1,256,1024]{3,2,1,0:T(8,128)(2,1)S(1)}, bf16[1,1,256,1024]{3,2,1,0:T(8,128)(2,1)}, u32[]{:S(2)}) %copy-start.2) | copy-done | bytes 524312
  4.1 0.0 copy-start.3
  4.1 0.7 copy-done.3
  4.8 93.8 %shard_map.68 = (bf16[4,256,512]{2,1,0:T(8,128)(2,1)S(1)}, bf16[1,1,256,512]{3,2,1,0:T(8,128)(2,1)S(1)}) custom-call(s32[1,4]{1,0:T(1,128)S(1)} %copy-done.3, bf16[4,256,512]{2,1,0:T(8,128)(2,1)S(1)} %copy-done, bf16[4,256,512]{2,1,0:T(8,128)(2,1)S(1)} %copy-done.1, bf16[4,256,512]{2,1,0:T(8,128)(2,1)} %w_ref.1, bf16[1,1,256,1024]{3,2,1,0:T(8,128)(2,1)S(1)} %copy-done.2), custom_call_target="tpu_custom_call" | custom-call | tf_op jit(solution)/shard_map/pallas_call | solution.py:209
  98.6 1.0 copy.9
  99.6 0.7 copy.10
Async XLA Ops:
  0.6 1.2 %copy-start = (bf16[4,256,512]{2,1,0:T(8,128)(2,1)S(1)}, bf16[4,256,512]{2,1,0:T(8,128)(2,1)}, u32[]{:S(2)}) copy-start(bf16[4,256,512]{2,1,0:T(8,128)(2,1)} %mom_ref.1) | copy-start | bytes 3145732
  1.9 1.2 %copy-start.1 = (bf16[4,256,512]{2,1,0:T(8,128)(2,1)S(1)}, bf16[4,256,512]{2,1,0:T(8,128)(2,1)}, u32[]{:S(2)}) copy-start(bf16[4,256,512]{2,1,0:T(8,128)(2,1)} %grad_ref.1) | copy-start | bytes 3145732
  3.1 1.0 %copy-start.2 = (bf16[1,1,256,1024]{3,2,1,0:T(8,128)(2,1)S(1)}, bf16[1,1,256,1024]{3,2,1,0:T(8,128)(2,1)}, u32[]{:S(2)}) copy-start(bf16[1,1,256,1024]{3,2,1,0:T(8,128)(2,1)} %tok_ref.1) | copy-start | bytes 1572868
  4.1 0.7 copy-start.3

commit v2 on v1

--- a/solution.py
+++ b/solution.py
@@ -18,9 +18,9 @@
 
 
 def kernel(
-    n, groups, slot_ref, mom_ref, grad_ref, w_ref, tok_ref, fresh_ref, hid_ref,
-    part, line_sums, group_sums, x_buf, gram_buf, poly_buf, w_buf, tok_buf, nw_buf, hid_send, hid_recv,
-    line_s, line_r, group_s, group_r, x_s, x_r, w_s, w_r, tok_s, tok_r, nw_s, nw_r, hid_s, hid_r,
+    n, groups, slot_ref, mom_hbm, grad_hbm, w_ref, tok_ref, fresh_ref, hid_ref,
+    mom_ref, grad_ref, part, line_sums, group_sums, x_buf, gram_buf, poly_buf, w_buf, tok_buf, nw_buf, hid_send, hid_recv,
+    load_s, line_s, line_r, group_s, group_r, x_s, x_r, w_s, w_r, tok_s, tok_r, pass_s, nw_s, nw_r, hid_s, hid_r,
 ):
     half = n // 2
     z, g = lax.axis_index("shard"), lax.axis_index("group")
@@ -59,6 +59,11 @@
     def landed(dst, rsem):
         pltpu.make_async_copy(dst, dst, rsem).wait()
 
+    load_grad = pltpu.make_async_copy(grad_hbm, grad_ref, load_s.at[0])
+    load_mom = pltpu.make_async_copy(mom_hbm, mom_ref, load_s.at[1])
+    load_grad.start()
+    load_mom.start()
+
     barrier = pltpu.get_barrier_semaphore()
 
     def greet(zz, gg):
@@ -70,6 +75,8 @@
             greet(lax.rem(z + step, n), g)
     for step in range(2, groups):
         greet(z, lax.rem(base + step, groups))
+
+    load_grad.wait()
 
     def squares(i, total):
         wide = grad_ref[i].astype(f32)
@@ -89,6 +96,23 @@
     for step in range(1, n):
         other = lax.rem(z + step, n)
         landed(line_sums.at[other], line_r.at[other])
+    first = core * half
+    entry = lax.clamp(first, z, first + half - 1)
+    token_copy = (tok_ref.at[0, 0], tok_buf.at[spot], tok_s, tok_r.at[spot], entry, base + side)
+
+    def passing(i, act):
+        low = side * half
+        enters = lax.clamp(low, core * half + i, low + half - 1)
+
+        @pl.when(jnp.logical_and(z <= enters, z > low))
+        def _():
+            act(remote(tok_buf.at[i], tok_buf.at[i], pass_s.at[0, i], tok_r.at[i], z - 1, g))
+
+        @pl.when(jnp.logical_and(z >= enters, z < low + half - 1))
+        def _():
+            act(remote(tok_buf.at[i], tok_buf.at[i], pass_s.at[1, i], tok_r.at[i], z + 1, g))
+
+    ship(*token_copy)
     part[1] = jnp.sum(line_sums[...], axis=0)
     for step in range(1, groups):
         to = lax.rem(g + step, groups)
@@ -111,11 +135,6 @@
     def weight_copy(j):
         return (w_ref.at[j], w_buf.at[my_rows], w_s.at[j], w_r.at[z], *owner(j))
 
-    slot_core = base + side
-
-    def token_copy(i):
-        return (tok_ref.at[0, 0], tok_buf.at[spot], tok_s.at[i], tok_r.at[spot], core * half + i, slot_core)
-
     def every(count, act):
         def body(i, carry):
             act(i)
@@ -127,9 +146,15 @@
         fresh_ref[j] = (momentum_decay * mom_ref[j].astype(f32) + clip * grad_ref[j].astype(f32)).astype(bf16)
         ship(*row_copy(j))
 
+    load_mom.wait()
     every(n, freshen)
     every(n, lambda j: ship(*weight_copy(j)))
-    every(half, lambda i: ship(*token_copy(i)))
+
+    def relay(i):
+        landed(tok_buf.at[i], tok_r.at[i])
+        passing(i, lambda copy: copy.start())
+
+    every(half, relay)
 
     def block(d):
         return pl.ds(pl.multiple_of(d * rows, rows), rows)
@@ -163,23 +188,25 @@
 
     every(ITERS, iterate)
 
-    every(n, lambda d: landed(w_buf.at[block(d)], w_r.at[d]))
-
-    def renew(i):
-        at = pl.ds(pl.multiple_of(i * chunk, chunk), chunk)
+    def swap(d):
+        at = block(d)
+        return remote(nw_buf.at[core, at], nw_buf.at[core, at], nw_s.at[d], nw_r.at[d], z, base + 1 - core)
+
+    def renew(step):
+        d = lax.rem(z + step, n)
+        at = block(d)
         update = (0.2 * math.sqrt(depth) * x_buf[at].astype(f32)).astype(bf16)
+        landed(w_buf.at[at], w_r.at[d])
         nw_buf[core, at] = (w_buf[at].astype(f32) - learning_rate * update.astype(f32)).astype(bf16)
-
-    every(depth // chunk, renew)
-    swap = remote(nw_buf.at[core], nw_buf.at[core], nw_s, nw_r.at[core], z, base + 1 - core)
-    swap.start()
-    landed(nw_buf.at[1 - core], nw_r.at[1 - core])
+        swap(d).start()
+
+    every(n, renew)
+    every(n, lambda d: landed(nw_buf.at[1 - core, block(d)], nw_r.at[d]))
 
     def hidden_copy(i):
         return (hid_send.at[i], hid_recv.at[spot], hid_s.at[i], hid_r.at[spot], core * half + i, base + side)
 
     def prefill(i):
-        landed(tok_buf.at[i], tok_r.at[i])
         prompt = tok_buf[i]
         gate = jnp.dot(prompt, nw_buf[0], preferred_element_type=f32)
         up = jnp.dot(prompt, nw_buf[1], preferred_element_type=f32)
@@ -196,9 +223,10 @@
         remote(part.at[1], group_sums.at[g], group_s.at[step], group_r.at[g], z, lax.rem(g + step, groups)).wait_send()
     every(n, lambda j: sent(*row_copy(j)))
     every(n, lambda j: sent(*weight_copy(j)))
-    every(half, lambda i: sent(*token_copy(i)))
+    sent(*token_copy)
+    every(half, lambda i: passing(i, lambda copy: copy.wait_send()))
     every(half, lambda i: sent(*hidden_copy(i)))
-    swap.wait_send()
+    every(n, lambda d: swap(d).wait_send())
 
 
 def local(n, groups, momentum, gradient, weights, slot_map, tokens):
@@ -212,9 +240,11 @@
             jax.ShapeDtypeStruct(momentum.shape, bf16),
             jax.ShapeDtypeStruct((1, 1, prompts, cols), bf16),
         ),
-        in_specs=[pl.BlockSpec(memory_space=pltpu.SMEM)] + [vmem] * 4,
+        in_specs=[pl.BlockSpec(memory_space=pltpu.SMEM)] + [pl.BlockSpec(memory_space=pl.ANY)] * 4,
         out_specs=(vmem, vmem),
         scratch_shapes=[
+            pltpu.VMEM(momentum.shape, bf16),
+            pltpu.VMEM(momentum.shape, bf16),
             pltpu.VMEM((2, 8, 128), f32),
             pltpu.VMEM((n, 8, 128), f32),
             pltpu.VMEM((groups, 8, 128), f32),
@@ -226,12 +256,12 @@
             pltpu.VMEM((2, depth, cols), bf16),
             pltpu.VMEM((half, prompts, cols), bf16),
             pltpu.VMEM((half, prompts, cols), bf16),
-            dma((n,)), dma((n,)), dma((groups,)), dma((groups,)),
-            dma((n,)), dma((n,)), dma((n,)), dma((n,)), dma((half,)), dma((half,)),
-            dma(()), dma((2,)), dma((half,)), dma((half,)),
+            dma((2,)), dma((n,)), dma((n,)), dma((groups,)), dma((groups,)),
+            dma((n,)), dma((n,)), dma((n,)), dma((n,)), dma(()), dma((half,)), dma((2, half)),
+            dma((n,)), dma((n,)), dma((half,)), dma((half,)),
         ],
         compiler_params=pltpu.CompilerParams(
-            collective_id=0, has_side_effects=True, vmem_limit_bytes=50 * 2**20
+            collective_id=0, has_side_effects=True, vmem_limit_bytes=62 * 2**20
         ),
     )(slot_map, momentum, gradient, weights, tokens)
 

time: 101 us -> 92.7 us (0.918)
  Pallas kernels: 93.8 us -> 88.8 us
  local copies, waits for them, and re-layouts: 5.81 us -> 3.01 us
    pallas_call x1, Pallas kernels: 93.8 us -> 88.8 us  [local(): pl.pallas_call(functools.partial(kernel, n, groups), out_shape=(jax.Shape...]
    unnamed x10 -> x4, local copies, waits for them, and re-layouts: 5.81 us -> 3.01 us
where the time goes in v2:
time: 92.7 us; the launch traced here: 92.5 us
  Pallas kernels  88.8 us (96%)
  local copies, waits for them, and re-layouts  3.01 us (3%)
    pallas_call x1, Pallas kernels, local(): pl.pallas_call(functools.partial(kernel, n, groups), out_shape=(jax.Shape...  88.8 us
    unnamed x4, local copies, waits for them, and re-layouts  3.01 us

profile of v2, /device:TPU:9, one launch (start us, length us, event | category | flops | bytes accessed | tf_op | source)
XLA Modules:
  0.0 92.5 jit_solution(11152635370139258670)
XLA Ops:
  0.6 88.8 %shard_map.68 = (bf16[4,256,512]{2,1,0:T(8,128)(2,1)}, bf16[1,1,256,512]{3,2,1,0:T(8,128)(2,1)}) custom-call(s32[1,4]{1,0:T(1,128)} %slot_ref.1, bf16[4,256,512]{2,1,0:T(8,128)(2,1)} %mom_hbm.1, bf16[4,256,512]{2,1,0:T(8,128)(2,1)} %grad_hbm.1, bf16[4,256,512]{2,1,0:T(8,128)(2,1)} %w_ref.1, bf16[1,1,256,1024]{3,2,1,0:T(8,128)(2,1)} %tok_ref.1), custom_call_target="tpu_custom_call" | custom-call | tf_op jit(solution)/shard_map/pallas_call | solution.py:237
  89.5 0.0 copy-start
  89.5 2.3 %copy.9 = bf16[4,256,512]{2,1,0:T(8,128)(2,1)} copy(bf16[4,256,512]{2,1,0:T(8,128)(2,1)} %get-tuple-element.4) | data formatting | bytes 2097152
  91.8 0.0 copy-done
  91.8 0.7 copy.10
Async XLA Ops:
  89.5 2.3 %copy-start = (bf16[1,1,256,512]{3,2,1,0:T(8,128)(2,1)S(1)}, bf16[1,1,256,512]{3,2,1,0:T(8,128)(2,1)}, u32[]{:S(2)}) copy-start(bf16[1,1,256,512]{3,2,1,0:T(8,128)(2,1)} %get-tuple-element.5) | copy-start | bytes 786436

commit v3 on v2

--- a/solution.py
+++ b/solution.py
@@ -148,7 +148,7 @@
 
     load_mom.wait()
     every(n, freshen)
-    every(n, lambda j: ship(*weight_copy(j)))
+    every(half, lambda j: ship(*weight_copy(2 * j)))
 
     def relay(i):
         landed(tok_buf.at[i], tok_r.at[i])
@@ -160,6 +160,7 @@
         return pl.ds(pl.multiple_of(d * rows, rows), rows)
 
     every(n, lambda d: landed(x_buf.at[block(d)], x_r.at[d]))
+    every(half, lambda j: ship(*weight_copy(2 * j + 1)))
 
     chunk = 256
 

time: 92.7 us -> 88.7 us (0.957)
  Pallas kernels: 88.8 us -> 84.8 us
    pallas_call x1, Pallas kernels: 88.8 us -> 84.8 us  [local(): pl.pallas_call(functools.partial(kernel, n, groups), out_shape=(jax.Shape...]
where the time goes in v3:
time: 88.7 us; the launch traced here: 88.5 us
  Pallas kernels  84.8 us (96%)
  local copies, waits for them, and re-layouts  3.01 us (3%)
    pallas_call x1, Pallas kernels, local(): pl.pallas_call(functools.partial(kernel, n, groups), out_shape=(jax.Shape...  84.8 us
    unnamed x4, local copies, waits for them, and re-layouts  3.01 us

profile of v3, /device:TPU:9, one launch (start us, length us, event | category | flops | bytes accessed | tf_op | source)
XLA Modules:
  0.0 88.5 jit_solution(14151303085498966833)
XLA Ops:
  0.6 84.8 %shard_map.68 = (bf16[4,256,512]{2,1,0:T(8,128)(2,1)}, bf16[1,1,256,512]{3,2,1,0:T(8,128)(2,1)}) custom-call(s32[1,4]{1,0:T(1,128)} %slot_ref.1, bf16[4,256,512]{2,1,0:T(8,128)(2,1)} %mom_hbm.1, bf16[4,256,512]{2,1,0:T(8,128)(2,1)} %grad_hbm.1, bf16[4,256,512]{2,1,0:T(8,128)(2,1)} %w_ref.1, bf16[1,1,256,1024]{3,2,1,0:T(8,128)(2,1)} %tok_ref.1), custom_call_target="tpu_custom_call" | custom-call | tf_op jit(solution)/shard_map/pallas_call | solution.py:238
  85.5 0.0 copy-start
  85.5 2.3 %copy.9 = bf16[4,256,512]{2,1,0:T(8,128)(2,1)} copy(bf16[4,256,512]{2,1,0:T(8,128)(2,1)} %get-tuple-element.4) | data formatting | bytes 2097152
  87.8 0.0 copy-done
  87.8 0.7 copy.10
Async XLA Ops:
  85.5 2.3 %copy-start = (bf16[1,1,256,512]{3,2,1,0:T(8,128)(2,1)S(1)}, bf16[1,1,256,512]{3,2,1,0:T(8,128)(2,1)}, u32[]{:S(2)}) copy-start(bf16[1,1,256,512]{3,2,1,0:T(8,128)(2,1)} %get-tuple-element.5) | copy-start | bytes 786436

commit v4 on v2

--- a/solution.py
+++ b/solution.py
@@ -148,7 +148,7 @@
 
     load_mom.wait()
     every(n, freshen)
-    every(n, lambda j: ship(*weight_copy(j)))
+    every(half, lambda j: ship(*weight_copy(2 * j + 1)))
 
     def relay(i):
         landed(tok_buf.at[i], tok_r.at[i])
@@ -160,6 +160,7 @@
         return pl.ds(pl.multiple_of(d * rows, rows), rows)
 
     every(n, lambda d: landed(x_buf.at[block(d)], x_r.at[d]))
+    every(half, lambda j: ship(*weight_copy(2 * j)))
 
     chunk = 256
 

time: 92.7 us -> 87.8 us (0.947)
  Pallas kernels: 88.8 us -> 83.9 us
    pallas_call x1, Pallas kernels: 88.8 us -> 83.9 us  [local(): pl.pallas_call(functools.partial(kernel, n, groups), out_shape=(jax.Shape...]
where the time goes in v4:
time: 87.8 us; the launch traced here: 87.6 us
  Pallas kernels  83.9 us (96%)
  local copies, waits for them, and re-layouts  3.01 us (3%)
    pallas_call x1, Pallas kernels, local(): pl.pallas_call(functools.partial(kernel, n, groups), out_shape=(jax.Shape...  83.9 us
    unnamed x4, local copies, waits for them, and re-layouts  3.01 us

profile of v4, /device:TPU:9, one launch (start us, length us, event | category | flops | bytes accessed | tf_op | source)
XLA Modules:
  0.0 87.6 jit_solution(4555348441501374075)
XLA Ops:
  0.6 83.9 %shard_map.68 = (bf16[4,256,512]{2,1,0:T(8,128)(2,1)}, bf16[1,1,256,512]{3,2,1,0:T(8,128)(2,1)}) custom-call(s32[1,4]{1,0:T(1,128)} %slot_ref.1, bf16[4,256,512]{2,1,0:T(8,128)(2,1)} %mom_hbm.1, bf16[4,256,512]{2,1,0:T(8,128)(2,1)} %grad_hbm.1, bf16[4,256,512]{2,1,0:T(8,128)(2,1)} %w_ref.1, bf16[1,1,256,1024]{3,2,1,0:T(8,128)(2,1)} %tok_ref.1), custom_call_target="tpu_custom_call" | custom-call | tf_op jit(solution)/shard_map/pallas_call | solution.py:238
  84.6 0.0 copy-start
  84.6 2.3 %copy.9 = bf16[4,256,512]{2,1,0:T(8,128)(2,1)} copy(bf16[4,256,512]{2,1,0:T(8,128)(2,1)} %get-tuple-element.4) | data formatting | bytes 2097152
  86.9 0.0 copy-done
  86.9 0.7 copy.10
Async XLA Ops:
  84.6 2.3 %copy-start = (bf16[1,1,256,512]{3,2,1,0:T(8,128)(2,1)S(1)}, bf16[1,1,256,512]{3,2,1,0:T(8,128)(2,1)}, u32[]{:S(2)}) copy-start(bf16[1,1,256,512]{3,2,1,0:T(8,128)(2,1)} %get-tuple-element.5) | copy-start | bytes 786436
